TPU v7x, 32 devices: a whole 2x2x4 slice. The times are simulated.
32 devices in a mesh: bl: 8 (over z, y), ch: 4 (over x, core).
Axes of the slice: x: 2, y: 2, z: 4, core: 2. Of those that a mesh axis runs over, the one named last changes fastest.
Arguments:
- facet_grid: bfloat16 [4, 64, 16, 1024], P(None, None, None, 'ch'), may hold values from -2 to 2
- kernel: bfloat16 [16384, 1024], P('bl', 'ch'), may hold values from -0.1875 to 0.1875
- tile_of: int32 [32], P('bl'), may hold values from 0 to 3
- observed: bfloat16 [64, 2, 16384], P('ch', None, 'bl'), may hold values from -6 to 6
- flags: int32 [64, 16384], P('ch', 'bl'), may hold values 0 or 1
- pairs: int32 [2, 16384], P(None, 'bl'), may hold values from 0 to 511, as said below
- solver_order: int32 [512], replicated, may hold values from 0 to 511, as said below
Outputs:
- gains: float32 [64, 16, 512], P('ch', None, 'bl')
Inputs may be any that keep to these rules, and one draw needn't show every extreme that they name: `solver_order`: each station appears once. `pairs`: for row r, with j = (r mod 2048) // 256, the first station is solver_order[64 * j + m] for some m below 64; the second station differs from the first.
All inputs are finite; a program needn't handle non-finite values. No bound on the sum of `flags` on one device may be relied on, other than what follows from the above.
Results may differ from a plain program's by a relative error of at most 0.013.
Values may be sent and summed in bfloat16 or wider, within the bound.
A program may use at most 128 MiB of HBM per device.

v0:
```python
import jax
import jax.numpy as jnp
from jax import lax
from jax.sharding import PartitionSpec as P

S = 512
ND = 8
ITERS = 4


def extended(shard, sides, width):
    for axis, dim in sides:
        devices, length = (lax.axis_size(axis), shard.shape[dim])
        up = [(i, (i + 1) % devices) for i in range(devices - 1)]
        down = [(j, i) for i, j in up]
        last = lax.slice_in_dim(shard, length - width, length, axis=dim)
        initial = lax.slice_in_dim(shard, 0, width, axis=dim)
        before = lax.ppermute(last, axis, up)
        after = lax.ppermute(initial, axis, down)
        shard = jnp.concatenate([before, shard, after], axis=dim)
    return shard


def lookup(gain_flat, pick):
    return jnp.dot(
        gain_flat, pick, precision=lax.Precision.HIGHEST, preferred_element_type=jnp.float32
    )


def row_terms(model_vis, visible, far_gain, near_gain):
    channels = model_vis.shape[0]
    row_count = model_vis.shape[2]
    model_pair = model_vis.reshape(channels, ND, 2, row_count)
    model_re = model_pair[:, :, 0].astype(jnp.float32)
    model_im = model_pair[:, :, 1].astype(jnp.float32)
    far_pair = far_gain.reshape(channels, ND, 2, row_count)
    near_pair = near_gain.reshape(channels, ND, 2, row_count)
    far_re = far_pair[:, :, 0]
    far_im = far_pair[:, :, 1]
    near_re = near_pair[:, :, 0]
    near_im = near_pair[:, :, 1]
    prod_re = model_re * far_re + model_im * far_im
    prod_im = model_im * far_re - model_re * far_im
    pred_re = jnp.sum(near_re * prod_re - near_im * prod_im, axis=1)
    pred_im = jnp.sum(near_re * prod_im + near_im * prod_re, axis=1)
    resid_re = visible[:, 0].astype(jnp.float32) - pred_re
    resid_im = visible[:, 1].astype(jnp.float32) - pred_im
    cross_re = prod_re * resid_re[:, None, :] + prod_im * resid_im[:, None, :]
    cross_im = prod_re * resid_im[:, None, :] - prod_im * resid_re[:, None, :]
    power = prod_re * prod_re + prod_im * prod_im
    stacked = jnp.concatenate([cross_re, cross_im, power], axis=1)
    return stacked.reshape(channels * 3 * ND, row_count)


def update_gains(gain_shard, sum_re, sum_im, power):
    channels = gain_shard.shape[0]
    owned = gain_shard.shape[2]
    gain_pair = gain_shard.reshape(channels, ND, 2, owned)
    gain_re = gain_pair[:, :, 0]
    gain_im = gain_pair[:, :, 1]
    new_re = (sum_re + gain_re * power) / (power + 1.0)
    new_im = (sum_im + gain_im * power) / (power + 1.0)
    averaged = jnp.stack([(gain_re + new_re) * 0.5, (gain_im + new_im) * 0.5], axis=2).reshape(
        channels, 2 * ND, owned
    )
    padded = extended(averaged, (("ch", 0),), 1)
    total_channels = channels * lax.axis_size("ch")
    chan_index = lax.axis_index("ch") * channels + jnp.arange(channels, dtype=jnp.int32)
    has_left = (chan_index > 0).astype(jnp.float32)[:, None, None]
    has_right = (chan_index < total_channels - 1).astype(jnp.float32)[:, None, None]
    return (0.25 * has_left * padded[:-2] + 0.5 * padded[1:-1] + 0.25 * has_right * padded[2:]) / (
        0.5 + 0.25 * has_left + 0.25 * has_right
    )


def body(facet_grid, kernel, tile_of, observed, flags, pairs, solver_order):
    channels = observed.shape[0]
    row_count = observed.shape[2]
    cell_count = kernel.shape[1]
    tile_count = facet_grid.shape[0]
    block_count = tile_of.shape[0]
    block_rows = row_count // block_count
    tile_pick = (tile_of[:, None] == jnp.arange(tile_count, dtype=jnp.int32)[None, :]).astype(
        jnp.bfloat16
    )
    kernel_blocks = kernel.reshape(block_count, block_rows, cell_count)
    chosen = jnp.einsum(
        "bt,tckg->bckg", tile_pick, facet_grid, preferred_element_type=jnp.float32
    ).astype(jnp.bfloat16)
    partial_vis = jnp.einsum(
        "bckg,bvg->ckbv", chosen, kernel_blocks, preferred_element_type=jnp.float32
    )
    summed = lax.psum_scatter(
        partial_vis.reshape(channels * lax.axis_size("ch"), partial_vis.shape[1], row_count).astype(
            jnp.bfloat16
        ),
        "ch",
        scatter_dimension=0,
        tiled=True,
    ).astype(jnp.float32)
    kept_rows = (1 - flags).astype(jnp.float32)
    model_vis = (summed * kept_rows[:, None, :]).astype(jnp.bfloat16)
    visible = (observed.astype(jnp.float32) * kept_rows[:, None, :]).astype(jnp.bfloat16)
    inverse = jnp.zeros((S,), jnp.int32).at[solver_order].set(jnp.arange(S, dtype=jnp.int32))
    bl_count = lax.axis_size("bl")
    owned = S // bl_count
    station_ids = jnp.arange(S, dtype=jnp.int32)[:, None]
    packed = pairs.reshape(1, 2, row_count)
    model_vis, visible, packed = (
        lax.all_to_all(model_vis, "bl", split_axis=2, concat_axis=2, tiled=True),
        lax.all_to_all(visible, "bl", split_axis=2, concat_axis=2, tiled=True),
        lax.all_to_all(packed, "bl", split_axis=2, concat_axis=2, tiled=True),
    )
    first_slot = inverse[packed[0, 0]]
    second_slot = inverse[packed[0, 1]]
    owner_slot = first_slot - lax.axis_index("bl") * owned
    near_pick = (owner_slot[None, :] == jnp.arange(owned, dtype=jnp.int32)[:, None]).astype(
        jnp.float32
    )
    far_pick = (second_slot[None, :] == station_ids).astype(jnp.float32)
    gain_shard = (
        jnp.zeros((channels, ND, 2, owned), jnp.float32)
        .at[:, :, 0, :]
        .set(1.0)
        .reshape(channels, 2 * ND, owned)
    )
    all_gains = (
        jnp.zeros((channels, ND, 2, S), jnp.float32)
        .at[:, :, 0, :]
        .set(1.0)
        .reshape(channels, 2 * ND, S)
    )
    for iteration in range(ITERS):
        if iteration > 0:
            all_gains = lax.all_gather(gain_shard, "bl", axis=2, tiled=True)
        far_gain = lookup(all_gains.reshape(channels * 2 * ND, S), far_pick)
        near_gain = lookup(gain_shard.reshape(channels * 2 * ND, owned), near_pick)
        stacked = row_terms(model_vis, visible, far_gain, near_gain)
        station_terms = jnp.einsum(
            "fv,sv->fs",
            stacked,
            near_pick,
            precision=lax.Precision.HIGHEST,
            preferred_element_type=jnp.float32,
        )
        mine = station_terms.reshape(channels, 3 * ND, owned)
        sum_re = mine[:, :ND]
        sum_im = mine[:, ND : 2 * ND]
        sum_power = mine[:, 2 * ND :]
        gain_shard = update_gains(gain_shard, sum_re, sum_im, sum_power)
    return gain_shard


def solution(mesh):
    in_specs = (
        P(None, None, None, "ch"),
        P("bl", "ch"),
        P("bl"),
        P("ch", None, "bl"),
        P("ch", "bl"),
        P(None, "bl"),
        P(),
    )
    out_specs = P("ch", None, "bl")
    return jax.shard_map(body, mesh=mesh, in_specs=in_specs, out_specs=out_specs, check_vma=False)
```

profile of v0, /device:TPU:0, one launch (start us, length us, event | category | flops | bytes accessed | tf_op | source)
XLA Modules:
  0.0 569.5 jit_solution(13722925081417252668)
XLA Ops:
  8.1 2.4 fusion.41
  11.9 2.6 copy.184
  16.1 9.3 %reduce.8 = s32[2048,2]{1,0:T(8,128)S(1)} reduce(s32[2048,1,2]{2,1,0:T(1,128)S(1)} %bitcast.258, s32[]{:T(128)} %broadcast.242), dimensions={1}, to_apply=%bitcast.230.reduce_sub_computation | reduce | bytes 32772
  26.7 7.3 %all-to-all-start.1 = ((s32[8,1,512]{2,1,0:T(1,128)}), s32[8,1,512]{2,1,0:T(1,128)S(1)}, u32[]{:S(2)}, u32[]{:S(2)}) async-start(s32[8,1,512]{2,1,0:T(1,128)} %reshape.309), calls=%async_computation.2 | async-start | bytes 32768 | tf_op jit(solution)/shard_map/all_to_all | solution.py:112
  36.7 2.4 scatter_custom_fusion
  40.6 4.6 all-to-all-start.2
  47.6 114.5 %slice_reduce_fusion = (s32[2048]{0:T(1024)S(1)}, s32[2048]{0:T(1024)S(1)}) fusion(s32[1,2,2048]{1,0,2:T(1,128)S(1)} %bitcast.255), kind=kLoop, calls=%fused_computation.86 | loop fusion | bytes 32768 | tf_op jit(solution)/shard_map/slice | solution.py:114
  162.1 13.2 %gather_fusion.1 = s32[2048]{0:T(1024)S(1)} fusion(s32[512]{0:T(512)S(1)} %scatter_custom_fusion, s32[2048]{0:T(1024)S(1)} %broadcast_clamp_fusion), kind=kCustom, calls=%fused_computation.1 | custom fusion | bytes 24576 | tf_op jit(solution)/shard_map/gather | solution.py:114
  176.9 8.5 %copy.88 = bf16[16,16,2048]{1,0,2:T(8,128)(2,1)} copy(bf16[16,16,2048]{2,1,0:T(8,128)(2,1)S(1)} %multiply_convert_fusion) | data formatting | bytes 2097152 | tf_op jit(solution)/shard_map/convert_element_type | solution.py:102
  185.4 11.2 %reshape.311 = bf16[8,2,32768]{2,1,0:T(2,128)(2,1)} reshape(bf16[2048,16,16]{2,1,0:T(8,128)(2,1)} %bitcast.252) | data formatting | bytes 2097152
  196.6 6.2 %all-to-all-start = ((bf16[8,2,32768]{2,1,0:T(2,128)(2,1)}), bf16[8,2,32768]{2,1,0:T(2,128)(2,1)S(1)}, u32[]{:S(2)}, u32[]{:S(2)}) async-start(bf16[8,2,32768]{2,1,0:T(2,128)(2,1)} %reshape.311), calls=%async_computation.1 | async-start | bytes 2097152 | tf_op jit(solution)/shard_map/all_to_all | solution.py:110
  202.9 13.2 %gather_fusion = s32[2048]{0:T(1024)S(1)} fusion(s32[512]{0:T(512)S(1)} %scatter_custom_fusion, s32[2048]{0:T(1024)S(1)} %broadcast_clamp_fusion.1), kind=kCustom, calls=%fused_computation | custom fusion | bytes 24576 | tf_op jit(solution)/shard_map/gather | solution.py:115
  216.1 2.3 fusion.73
  218.5 3.4 fusion.8
  222.6 2.3 fusion.174
  227.6 7.5 %reshape.312 = bf16[2048,16,16]{2,1,0:T(8,128)(2,1)} reshape(bf16[8,2,32768]{2,1,0:T(2,128)(2,1)S(1)} %all-to-all-done) | data formatting | bytes 2097152
  235.2 9.1 %copy.89 = bf16[16,16,2048]{2,0,1:T(8,128)(2,1)S(1)} copy(bf16[16,16,2048]{1,0,2:T(8,128)(2,1)} %bitcast.253) | data formatting | bytes 2097152 | tf_op jit(solution)/shard_map/all_to_all | solution.py:110
  245.9 2.9 subtract_reduce_fusion.3
  253.7 3.4 collective-permute-done.1
  257.5 2.3 fusion.71
  260.0 83.7 %all_gather.9 = f32[16,16,512]{1,0,2:T(8,128)} all-gather(f32[16,16,64]{1,0,2:T(8,128)S(1)} %copy.110), channel_id=1, replica_groups=mesh['bl'=8,'ch'=4] {'bl'}, dimensions={2}, use_global_device_ids=true | all-gather | bytes 589824 | tf_op jit(solution)/shard_map/all_gather | solution.py:135
  343.7 3.2 copy.111
  352.7 3.5 collective-permute-start.2
  357.6 3.0 collective-permute-done.3
  361.0 2.3 fusion.69
  363.4 82.5 %all_gather.10 = f32[16,16,512]{1,0,2:T(8,128)} all-gather(f32[16,16,64]{1,0,2:T(8,128)S(1)} %copy.125), channel_id=1, replica_groups=mesh['bl'=8,'ch'=4] {'bl'}, dimensions={2}, use_global_device_ids=true | all-gather | bytes 589824 | tf_op jit(solution)/shard_map/all_gather | solution.py:135
  445.9 3.2 copy.126
  449.1 2.3 fusion.2
  460.7 2.3 fusion.67
  463.1 84.1 %all_gather.11 = f32[16,16,512]{1,0,2:T(8,128)} all-gather(f32[16,16,64]{1,0,2:T(8,128)S(1)} %copy.140), channel_id=1, replica_groups=mesh['bl'=8,'ch'=4] {'bl'}, dimensions={2}, use_global_device_ids=true | all-gather | bytes 589824 | tf_op jit(solution)/shard_map/all_gather | solution.py:135
  547.2 3.2 copy.141
  550.4 2.3 fusion.6
  (123 shorter events, 50.3 us)
Async XLA Ops:
  6.5 1.6 copy-start
  6.5 4.0 copy-start.6
  6.5 168.8 %reduce-scatter.2.cloned.1.call-start = ((), (), s32[]{:S(2)}) async-start(), calls=%async_computation.4 | async-start | bytes 5242880 | tf_op jit(solution)/shard_map/reduce_scatter | solution.py:93
  14.5 0.7 copy-start.10
  15.2 18.8 %copy-start.11 = (s32[512]{0:T(512)S(1)}, s32[512]{0:T(512)}, u32[]{:S(2)}) copy-start(s32[512]{0:T(512)} %param.17) | copy-start | bytes 6148
  15.2 18.8 %copy-start.9 = (s32[16,2048]{1,0:T(8,128)S(1)}, s32[16,2048]{1,0:T(8,128)}, u32[]{:S(2)}) copy-start(s32[16,2048]{1,0:T(8,128)} %param.15) | copy-start | bytes 393220
  15.2 18.9 %copy-start.7 = (bf16[16,2,2048]{2,1,0:T(2,128)(2,1)S(1)}, bf16[16,2,2048]{2,1,0:T(2,128)(2,1)}, u32[]{:S(2)}) copy-start(bf16[16,2,2048]{2,1,0:T(2,128)(2,1)} %param.14) | copy-start | bytes 393220
  26.7 13.9 %all-to-all-start.1 = ((s32[8,1,512]{2,1,0:T(1,128)}), s32[8,1,512]{2,1,0:T(1,128)S(1)}, u32[]{:S(2)}, u32[]{:S(2)}) async-start(s32[8,1,512]{2,1,0:T(1,128)} %reshape.309), calls=%async_computation.2 | async-start | bytes 32768 | tf_op jit(solution)/shard_map/all_to_all | solution.py:112
  40.6 156.1 %all-to-all-start.2 = ((bf16[8,2,4096]{2,1,0:T(2,128)(2,1)}), bf16[8,2,4096]{2,1,0:T(2,128)(2,1)S(1)}, u32[]{:S(2)}, u32[]{:S(2)}) async-start(bf16[8,2,4096]{2,1,0:T(2,128)(2,1)} %reshape.313), calls=%async_computation.3 | async-start | bytes 262144 | tf_op jit(solution)/shard_map/all_to_all | solution.py:111
  196.6 31.0 %all-to-all-start = ((bf16[8,2,32768]{2,1,0:T(2,128)(2,1)}), bf16[8,2,32768]{2,1,0:T(2,128)(2,1)S(1)}, u32[]{:S(2)}, u32[]{:S(2)}) async-start(bf16[8,2,32768]{2,1,0:T(2,128)(2,1)} %reshape.311), calls=%async_computation.1 | async-start | bytes 2097152 | tf_op jit(solution)/shard_map/all_to_all | solution.py:110
  202.9 13.3 %copy-start.8 = (f32[16,8,2,64]{3,1,0,2:T(8,128)S(1)}, f32[16,8,2,64]{3,1,0,2:T(8,128)}, u32[]{:S(2)}) copy-start(f32[16,8,2,64]{3,1,0,2:T(8,128)} %constant.98) | copy-start | bytes 196612
  202.9 15.6 %copy-start.12 = (f32[16,8,2,512]{3,1,2,0:T(8,128)S(1)}, f32[16,8,2,512]{3,1,2,0:T(8,128)}, u32[]{:S(2)}) copy-start(f32[16,8,2,512]{3,1,2,0:T(8,128)} %constant.89.clone.1) | copy-start | bytes 1572868
  244.3 1.6 copy-start.2
  251.0 2.7 collective-permute-start
  252.3 4.8 collective-permute-start.1
  346.8 2.3 copy-start.4
  352.7 4.9 collective-permute-start.2
  356.2 4.3 collective-permute-start.3
  449.1 2.3 copy-start.5
  455.0 3.6 collective-permute-start.4
  457.2 3.1 collective-permute-start.5
  550.4 2.3 copy-start.3
  554.2 8.0 %copy-start.1 = (bf16[4,64,16,256]{3,2,1,0:T(8,128)(2,1)S(1)}, bf16[4,64,16,256]{3,2,1,0:T(8,128)(2,1)}, u32[]{:S(2)}) copy-start(bf16[4,64,16,256]{3,2,1,0:T(8,128)(2,1)} %param.11) | copy-start | bytes 6291460
  556.3 3.4 collective-permute-start.6
  558.3 3.1 collective-permute-start.7
Sparse Core Ops, SparseCore 0:
  14.6 47.2 reduce-scatter.1
where the time goes:
time: 581 us; the launch traced here: 570 us
  blocking collectives  250 us (43%)
  local copies, waits for them, and re-layouts  210 us (36%)
  starting transfers between devices  32.2 us (6%)
  matrix products  29.6 us (5%)
  other arithmetic  21.5 us (4%)
  between operations  14.8 us (3%)
  waiting for transfers between devices  11.3 us (2%)
    all_gather x3, blocking collectives, body(): all_gains = lax.all_gather(gain_shard, 'bl', axis=2, tiled=True)  250 us
    slice x1, local copies, waits for them, and re-layouts, body(): first_slot = inverse[packed[0, 0]]  114 us
    unnamed x36, local copies, waits for them, and re-layouts  31.6 us
    dot_general x8, matrix products, lookup(): jnp.dot(gain_flat, pick, precision=lax.Precision.HIGHEST, preferred_eleme...  19.6 us
    gather x1, local copies, waits for them, and re-layouts, body(): first_slot = inverse[packed[0, 0]]  13.2 us
    gather x1, local copies, waits for them, and re-layouts, body(): second_slot = inverse[packed[0, 1]]  13.2 us
  transfers between devices with their start and end apart: 12, of which 6 were waited for; matrix products, arithmetic and copies ran while one was open for 34% of the time, Pallas kernels for 0%

commit v1 on v0

v1 whole, which is shorter than its diff:
```python
import functools

import jax
import jax.numpy as jnp
from jax import lax
from jax.experimental import pallas as pl
from jax.experimental.pallas import tpu as pltpu
from jax.sharding import PartitionSpec as P

ND = 8
NK = 2 * ND
ITERS = 4
MESH = pl.DeviceIdType.MESH
F32 = jnp.float32
BF16 = jnp.bfloat16
NN = (((1,), (0,)), ((), ()))
NT = (((1,), (1,)), ((), ()))


def dot(a, b, dims=NN):
    return lax.dot_general(a, b, dims, preferred_element_type=F32)


def one_hot_rows(n):
    row = lax.broadcasted_iota(jnp.int32, (n, n), 0)
    col = lax.broadcasted_iota(jnp.int32, (n, n), 1)
    chan = row // NK
    k = row % NK
    source = chan * NK + (k % ND) * 2 + k // ND
    return (col == source).astype(F32).astype(BF16)


def fused(
    n_bl, n_ch, tile_count,
    tile_of, facet, kern, obs, flags, pairs, order,
    out,
    chosen, send1, recv1, own, recv2, send3, recv3, recvp, far_pick, near_pick,
    gains, h_buf, edge, g_send, g_all, g_lookup,
    s1, r1, s2, r2, s3, r3, sp, rp, sg, rg, se, re,
):
    b = lax.axis_index("bl")
    c = lax.axis_index("ch")
    seg = pairs.shape[2]
    chans = flags.shape[1]
    rows = chans * NK
    owned = out.shape[2]
    blocks = chosen.shape[0]
    segs_per_block = n_bl // blocks if n_bl >= blocks else 1
    par = lax.rem(c, 2)
    hi = lax.div(c, 2)
    mate = c + 1 - 2 * par
    across = (1 - hi) * 2 + par
    right = lax.rem(c + 1, n_ch)
    left = lax.rem(c + n_ch - 1, n_ch)

    def at(i):
        return lax.rem(b + 1 + i, n_bl)

    def back(i):
        return lax.rem(b + 2 * n_bl - 1 - i, n_bl)

    barrier = pltpu.get_barrier_semaphore()
    for step in range(1, n_ch):
        pl.semaphore_signal(
            barrier, inc=1, device_id={"ch": lax.rem(c + step, n_ch)}, device_id_type=MESH
        )

    def greet(i, carry):
        pl.semaphore_signal(barrier, inc=1, device_id={"bl": at(i)}, device_id_type=MESH)
        return carry

    lax.fori_loop(0, n_bl - 1, greet, 0)

    perm = one_hot_rows(rows)
    for block in range(blocks):
        tile = tile_of[block]
        for q in range(n_ch):
            pick = facet[0, q]
            for t in range(1, tile_count):
                pick = jnp.where(tile == t, facet[t, q], pick)
            chosen[block, q] = dot(perm, pick).astype(BF16)

    pl.semaphore_wait(barrier, n_ch - 1 + n_bl - 1)

    def pair_copy(src, dst, sem_s, sem_r, peer):
        return pltpu.make_async_remote_copy(
            src_ref=pairs.at[src], dst_ref=recvp.at[dst], send_sem=sp.at[sem_s],
            recv_sem=rp.at[sem_r], device_id={"bl": peer}, device_id_type=MESH,
        )

    def copy1(j):
        return pltpu.make_async_remote_copy(
            src_ref=send1.at[j], dst_ref=recv1.at[j], send_sem=s1.at[j], recv_sem=r1.at[j],
            device_id={"ch": mate}, device_id_type=MESH,
        )

    def copy2(j):
        return pltpu.make_async_remote_copy(
            src_ref=own.at[j, 1 - hi], dst_ref=recv2.at[j], send_sem=s2.at[j], recv_sem=r2.at[j],
            device_id={"ch": across}, device_id_type=MESH,
        )

    def copy3(src, dst, sem_s, sem_r, peer):
        return pltpu.make_async_remote_copy(
            src_ref=send3.at[src], dst_ref=recv3.at[dst], send_sem=s3.at[sem_s],
            recv_sem=r3.at[sem_r], device_id={"bl": peer}, device_id_type=MESH,
        )

    def gain_copy(it, dst, sem_s, sem_r, peer):
        return pltpu.make_async_remote_copy(
            src_ref=g_send.at[it], dst_ref=g_all.at[it, dst], send_sem=sg.at[it, sem_s],
            recv_sem=rg.at[it, sem_r], device_id={"bl": peer}, device_id_type=MESH,
        )

    def edge_copy(it, side):
        return pltpu.make_async_remote_copy(
            src_ref=h_buf.at[it, (chans - 1) * (1 - side)], dst_ref=edge.at[it, side],
            send_sem=se.at[it, side], recv_sem=re.at[it, side],
            device_id={"ch": right if side == 0 else left}, device_id_type=MESH,
        )

    def send_pairs(i, carry):
        j = at(i)
        pair_copy(j, b, j, b, j).start()
        return carry

    lax.fori_loop(0, n_bl - 1, send_pairs, 0)

    def first(i, carry):
        j = at(i)
        weights = kern[j]
        block = lax.div(j, segs_per_block)
        for half in range(2):
            send1[j, half] = dot(chosen[block, 2 * half + 1 - par], weights, NT).astype(BF16)
        copy1(j).start()
        for half in range(2):
            own[j, half] = dot(chosen[block, 2 * half + par], weights, NT).astype(BF16)
        return carry

    lax.fori_loop(0, n_bl, first, 0)

    def second(i, carry):
        j = at(i)
        copy1(j).wait_recv()
        total = own[j, 1 - hi].astype(F32) + recv1[j, 1 - hi].astype(F32)
        own[j, 1 - hi] = total.astype(BF16)
        copy2(j).start()
        return carry

    lax.fori_loop(0, n_bl, second, 0)

    def picks(s):
        far_pick[s] = (order[...] == recvp[s, 1:2]).astype(F32).astype(BF16)
        mine = order[pl.ds(pl.multiple_of(b * owned, owned), owned)]
        near_pick[s] = (mine == recvp[s, 0:1]).astype(F32).astype(BF16)

    recvp[b] = pairs[b]
    picks(b)

    def take_pairs(i, carry):
        s = back(i)
        pair_copy(b, s, s, s, s).wait_recv()
        picks(s)
        return carry

    lax.fori_loop(0, n_bl - 1, take_pairs, 0)

    def finish(j, target, slot):
        copy2(j).wait_recv()
        kept = (1 - flags[j]).astype(F32)
        total = own[j, hi].astype(F32) + recv1[j, hi].astype(F32) + recv2[j].astype(F32)
        model = total.reshape(chans, NK, seg) * kept[:, None, :]
        target[slot, :rows] = model.reshape(rows, seg).astype(BF16)
        for part in range(2):
            seen = obs[j, part * chans : (part + 1) * chans].astype(F32) * kept
            target[slot, rows + part * chans : rows + (part + 1) * chans] = seen.astype(BF16)

    def third(i, carry):
        j = at(i)
        finish(j, send3, j)
        copy3(j, b, j, b, j).start()
        return carry

    lax.fori_loop(0, n_bl - 1, third, 0)
    finish(b, recv3, b)

    part = lax.broadcasted_iota(jnp.int32, (chans, NK, owned), 1)
    gains[...] = (part < ND).astype(F32)

    chan = lax.broadcasted_iota(jnp.int32, (chans, NK, owned), 0) + c * chans
    has_left = (chan > 0).astype(F32) * 0.25
    has_right = (chan < n_ch * chans - 1).astype(F32) * 0.25

    def terms(it, s, near_hi, near_lo):
        near_one = near_pick[s]
        model = recv3[s, :rows].astype(F32).reshape(chans, NK, seg)
        model_re, model_im = model[:, :ND], model[:, ND:]
        if it == 0:
            prod_re, prod_im = model_re, model_im
            pred_re = jnp.sum(prod_re, axis=1)
            pred_im = jnp.sum(prod_im, axis=1)
        else:
            far = dot(g_lookup[...], far_pick[s]).reshape(chans, NK, seg)
            near = (dot(near_hi, near_one) + dot(near_lo, near_one)).reshape(chans, NK, seg)
            far_re, far_im = far[:, :ND], far[:, ND:]
            near_re, near_im = near[:, :ND], near[:, ND:]
            prod_re = model_re * far_re + model_im * far_im
            prod_im = model_im * far_re - model_re * far_im
            pred_re = jnp.sum(near_re * prod_re - near_im * prod_im, axis=1)
            pred_im = jnp.sum(near_re * prod_im + near_im * prod_re, axis=1)
        res_re = (recv3[s, rows : rows + chans].astype(F32) - pred_re)[:, None, :]
        res_im = (recv3[s, rows + chans : rows + 2 * chans].astype(F32) - pred_im)[:, None, :]
        cross_re = prod_re * res_re + prod_im * res_im
        cross_im = prod_re * res_im - prod_im * res_re
        power = prod_re * prod_re + prod_im * prod_im
        cross = jnp.concatenate([cross_re, cross_im], axis=1).reshape(rows, seg).astype(BF16)
        power = power.reshape(chans * ND, seg).astype(BF16)
        return dot(cross, near_one, NT), dot(power, near_one, NT)

    for it in range(ITERS):
        near_hi = near_lo = None
        if it > 0:
            flat = gains[...].reshape(rows, owned)
            near_hi = flat.astype(BF16)
            near_lo = (flat - near_hi.astype(F32)).astype(BF16)

            def take_gains(i, carry):
                s = back(i)
                gain_copy(it - 1, s, s, s, s).wait_recv()
                return carry

            lax.fori_loop(0, n_bl - 1, take_gains, 0)
            table = g_all[it - 1].astype(F32).reshape(n_bl * owned, rows)
            g_lookup[...] = table.T.astype(BF16)

        def one(i, sums):
            s = back(i)
            if it == 0:

                @pl.when(i < n_bl - 1)
                def _():
                    copy3(s, s, s, s, s).wait_recv()

            more = terms(it, s, near_hi, near_lo)
            return sums[0] + more[0], sums[1] + more[1]

        zeros = (jnp.zeros((rows, owned), F32), jnp.zeros((chans * ND, owned), F32))
        cross, power = lax.fori_loop(0, n_bl, one, zeros)
        gain = gains[...]
        cross = cross.reshape(chans, NK, owned)
        power = power.reshape(chans, ND, owned)
        power = jnp.concatenate([power, power], axis=1)
        h_buf[it] = (gain + (cross + gain * power) / (power + 1.0)) * 0.5
        for side in range(2):
            edge_copy(it, side).start()
        for side in range(2):
            edge_copy(it, side).wait_recv()
        here = h_buf[it]
        before = jnp.concatenate([edge[it, 0:1], here[:-1]], axis=0)
        after = jnp.concatenate([here[1:], edge[it, 1:2]], axis=0)
        gain = (has_left * before + 0.5 * here + has_right * after) / (0.5 + has_left + has_right)
        if it == ITERS - 1:
            out[...] = gain
        else:
            gains[...] = gain
            turned = gain.reshape(rows, owned).T.astype(g_send.dtype)
            g_send[it] = turned

            def spread(i, carry):
                j = at(i)
                gain_copy(it, b, j, b, j).start()
                return carry

            lax.fori_loop(0, n_bl - 1, spread, 0)
            g_all[it, b] = turned

    for it in range(ITERS):
        for side in range(2):
            edge_copy(it, side).wait_send()

    def drain(i, carry):
        j = at(i)
        pair_copy(j, b, j, b, j).wait_send()
        copy3(j, b, j, b, j).wait_send()
        for it in range(ITERS - 1):
            gain_copy(it, b, j, b, j).wait_send()
        return carry

    lax.fori_loop(0, n_bl - 1, drain, 0)

    def drain_sums(j, carry):
        copy1(j).wait_send()
        copy2(j).wait_send()
        return carry

    lax.fori_loop(0, n_bl, drain_sums, 0)


def body(n_bl, n_ch, facet_grid, kernel, tile_of, observed, flags, pairs, solver_order):
    chans = observed.shape[0]
    row_count = observed.shape[2]
    seg = row_count // n_bl
    stations = solver_order.shape[0]
    owned = stations // n_bl
    cells = kernel.shape[1]
    tiles = facet_grid.shape[0]
    blocks = tile_of.shape[0]
    rows = chans * NK
    gdt = BF16 if owned % 16 == 0 else F32
    facet = facet_grid.reshape(tiles, n_ch, rows, cells)
    kern = kernel.reshape(n_bl, seg, cells)
    obs = observed.reshape(chans, 2, n_bl, seg).transpose(2, 1, 0, 3).reshape(n_bl, 2 * chans, seg)
    flag = flags.reshape(chans, n_bl, seg).transpose(1, 0, 2)
    pair = pairs.reshape(2, n_bl, seg).transpose(1, 0, 2)
    vmem = pl.BlockSpec(memory_space=pltpu.VMEM)
    dma = pltpu.SemaphoreType.DMA
    gains = pl.pallas_call(
        functools.partial(fused, n_bl, n_ch, tiles),
        out_shape=jax.ShapeDtypeStruct((chans, NK, owned), F32),
        in_specs=[pl.BlockSpec(memory_space=pltpu.SMEM)] + [vmem] * 6,
        out_specs=vmem,
        scratch_shapes=[
            pltpu.VMEM((blocks, n_ch, rows, cells), BF16),
            pltpu.VMEM((n_bl, 2, rows, seg), BF16),
            pltpu.VMEM((n_bl, 2, rows, seg), BF16),
            pltpu.VMEM((n_bl, 2, rows, seg), BF16),
            pltpu.VMEM((n_bl, rows, seg), BF16),
            pltpu.VMEM((n_bl, rows + 2 * chans, seg), BF16),
            pltpu.VMEM((n_bl, rows + 2 * chans, seg), BF16),
            pltpu.VMEM((n_bl, 2, seg), jnp.int32),
            pltpu.VMEM((n_bl, stations, seg), BF16),
            pltpu.VMEM((n_bl, owned, seg), BF16),
            pltpu.VMEM((chans, NK, owned), F32),
            pltpu.VMEM((ITERS, chans, NK, owned), F32),
            pltpu.VMEM((ITERS, 2, NK, owned), F32),
            pltpu.VMEM((ITERS - 1, owned, rows), gdt),
            pltpu.VMEM((ITERS - 1, n_bl, owned, rows), gdt),
            pltpu.VMEM((rows, stations), BF16),
        ]
        + [dma((n_bl,))] * 8
        + [dma((ITERS - 1, n_bl))] * 2
        + [dma((ITERS, 2))] * 2,
        compiler_params=pltpu.CompilerParams(
            collective_id=0, has_side_effects=True, vmem_limit_bytes=60 * 1024 * 1024
        ),
        name="calibrate",
    )(tile_of, facet, kern, obs, flag, pair, solver_order.reshape(stations, 1))
    return gains.reshape(chans, 2, ND, owned).transpose(0, 2, 1, 3).reshape(chans, NK, owned)


def solution(mesh):
    in_specs = (
        P(None, None, None, "ch"),
        P("bl", "ch"),
        P("bl"),
        P("ch", None, "bl"),
        P("ch", "bl"),
        P(None, "bl"),
        P(),
    )
    out_specs = P("ch", None, "bl")
    local = functools.partial(body, mesh.shape["bl"], mesh.shape["ch"])
    return jax.shard_map(local, mesh=mesh, in_specs=in_specs, out_specs=out_specs, check_vma=False)
```

time: 581 us -> 96.3 us (0.17); the launches traced: 570 us -> 96.1 us
  blocking collectives: 250 us -> 0 us
  local copies, waits for them, and re-layouts: 210 us -> 6.41 us
  Pallas kernels: 0 us -> 89.7 us
  starting transfers between devices: 32.2 us -> 0 us
  matrix products: 29.6 us -> 0 us
  other arithmetic: 21.5 us -> 0 us
  between operations: 14.8 us -> 0.01 us
  waiting for transfers between devices: 11.3 us -> 0 us
    all_gather x3 -> x0, blocking collectives: 250 us -> none  [body(): all_gains = lax.all_gather(gain_shard, 'bl', axis=2, tiled=True)]
    slice x11 -> x0, local copies, waits for them, and re-layouts: 117 us -> none  [the longest x1 114 us: body(): first_slot = inverse[packed[0, 0]]]
    pallas_call x0 -> x1, Pallas kernels: none -> 89.7 us  [body(): pl.pallas_call(functools.partial(fused, n_bl, n_ch, tiles), out_shape=jax...]
    unnamed x36 -> x0, local copies, waits for them, and re-layouts: 31.6 us -> none
    dot_general x14 -> x0, matrix products: 29.6 us -> none  [the longest x8 19.6 us: lookup(): jnp.dot(gain_flat, pick, precision=lax.Precision.HIGHEST, preferred_eleme...]
    gather x2 -> x0, local copies, waits for them, and re-layouts: 26.4 us -> none  [the longest x1 13.2 us: body(): first_slot = inverse[packed[0, 0]]]
    all_to_all x3 -> x0, starting transfers between devices: 18.1 us -> none  [the longest x1 7.28 us: body(): lax.all_to_all(packed, 'bl', split_axis=2, concat_axis=2, tiled=True)]
    ppermute x8 -> x0, starting transfers between devices: 14.1 us -> none  [the longest x4 8.98 us: extended(): before = lax.ppermute(last, axis, up)]
  transfers between devices with their start and end apart: 12 -> 0, of which waited for: 6 -> 0; matrix products, arithmetic and copies ran while one was open for 34% -> 0% of each run, Pallas kernels for 0% -> 0%
where the time goes in v1:
time: 96.3 us; the launch traced here: 96.1 us
  Pallas kernels  89.7 us (93%)
  local copies, waits for them, and re-layouts  6.41 us (7%)
    pallas_call x1, Pallas kernels, body(): pl.pallas_call(functools.partial(fused, n_bl, n_ch, tiles), out_shape=jax...  89.7 us

profile of v1, /device:TPU:0, one launch (start us, length us, event | category | flops | bytes accessed | tf_op | source)
XLA Modules:
  0.0 96.1 jit_solution(17478270906372276101)
XLA Ops:
  0.0 1.0 %reshape.29 = bf16[16,2,8,256]{3,2,1,0:T(8,128)(2,1)S(1)} reshape(bf16[16,2,2048]{2,1,0:T(2,128)(2,1)} %param.10) | data formatting | bytes 262144 | tf_op jit(solution)/shard_map/reshape | solution.py:312
  1.0 0.7 copy.10
  1.7 1.6 %copy.16 = s32[2,8,8,256]{3,2,0,1:T(8,128)} copy(s32[2,8,8,256]{3,2,1,0:T(8,128)} %bitcast.25) | data formatting | bytes 262144 | tf_op jit(solution)/shard_map/reshape | solution.py:313
  3.3 1.5 %copy.12.order = s32[512,1]{1,0:T(8,128)} copy(s32[512,1]{0,1:T(1,128)} %bitcast.27) | data formatting | bytes 4096 | tf_op jit(solution)/shard_map/reshape | solution.py:347
  4.8 89.7 %calibrate.1 = f32[16,16,64]{2,1,0:T(8,128)} custom-call(s32[4]{0:T(128)} %tile_of.1, bf16[4,4,256,256]{3,2,1,0:T(8,128)(2,1)} %bitcast.20, bf16[8,256,256]{2,1,0:T(8,128)(2,1)} %bitcast.21, bf16[8,32,256]{2,1,0:T(8,128)(2,1)} %bitcast.22, s32[8,16,256]{2,1,0:T(8,128)} %bitcast.24, s32[8,2,256]{2,1,0:T(2,128)} %bitcast.26, s32[512,1]{1,0:T(8,128)} %copy.12.order), custom_call_target="tpu_custom_call" | custom-call | tf_op jit(solution)/shard_map/calibrate/pallas_call | solution.py:317
  94.5 1.6 %copy.13 = f32[16,8,2,64]{3,2,1,0:T(2,128)} copy(f32[16,8,2,64]{3,1,2,0:T(8,128)} %bitcast.23) | data formatting | bytes 131072 | tf_op jit(solution)/shard_map/transpose | solution.py:348

commit v2 on v1

--- a/solution.py
+++ b/solution.py
@@ -32,10 +32,10 @@
 
 def fused(
     n_bl, n_ch, tile_count,
-    tile_of, facet, kern, obs, flags, pairs, order,
+    tile_of, facet, kern, obs, flags, pairs, order_row,
     out,
     chosen, send1, recv1, own, recv2, send3, recv3, recvp, far_pick, near_pick,
-    gains, h_buf, edge, g_send, g_all, g_lookup,
+    gains, h_buf, edge, g_all, g_lookup, order,
     s1, r1, s2, r2, s3, r3, sp, rp, sg, rg, se, re,
 ):
     b = lax.axis_index("bl")
@@ -71,6 +71,15 @@
 
     lax.fori_loop(0, n_bl - 1, greet, 0)
 
+    width = min(128, order_row.shape[1])
+    diagonal = lax.broadcasted_iota(jnp.int32, (width, width), 0) == lax.broadcasted_iota(
+        jnp.int32, (width, width), 1
+    )
+    for start in range(0, order_row.shape[1], width):
+        line = order_row[:, start : start + width].astype(F32)
+        column = jnp.sum(jnp.where(diagonal, line, 0.0), axis=1, keepdims=True)
+        order[start : start + width] = column.astype(jnp.int32)
+
     perm = one_hot_rows(rows)
     for block in range(blocks):
         tile = tile_of[block]
@@ -106,10 +115,10 @@
             recv_sem=r3.at[sem_r], device_id={"bl": peer}, device_id_type=MESH,
         )
 
-    def gain_copy(it, dst, sem_s, sem_r, peer):
-        return pltpu.make_async_remote_copy(
-            src_ref=g_send.at[it], dst_ref=g_all.at[it, dst], send_sem=sg.at[it, sem_s],
-            recv_sem=rg.at[it, sem_r], device_id={"bl": peer}, device_id_type=MESH,
+    def gain_copy(it, held, sem_s, peer):
+        return pltpu.make_async_remote_copy(
+            src_ref=g_all.at[it, held], dst_ref=g_all.at[it, held], send_sem=sg.at[it, sem_s],
+            recv_sem=rg.at[it, held], device_id={"bl": peer}, device_id_type=MESH,
         )
 
     def edge_copy(it, side):
@@ -152,6 +161,7 @@
     def picks(s):
         far_pick[s] = (order[...] == recvp[s, 1:2]).astype(F32).astype(BF16)
         mine = order[pl.ds(pl.multiple_of(b * owned, owned), owned)]
+        mine = jnp.concatenate([mine, mine], axis=0)
         near_pick[s] = (mine == recvp[s, 0:1]).astype(F32).astype(BF16)
 
     recvp[b] = pairs[b]
@@ -191,8 +201,9 @@
     has_left = (chan > 0).astype(F32) * 0.25
     has_right = (chan < n_ch * chans - 1).astype(F32) * 0.25
 
-    def terms(it, s, near_hi, near_lo):
-        near_one = near_pick[s]
+    def terms(it, s, near_gain):
+        near_two = near_pick[s]
+        near_one = near_two[:owned]
         model = recv3[s, :rows].astype(F32).reshape(chans, NK, seg)
         model_re, model_im = model[:, :ND], model[:, ND:]
         if it == 0:
@@ -201,7 +212,7 @@
             pred_im = jnp.sum(prod_im, axis=1)
         else:
             far = dot(g_lookup[...], far_pick[s]).reshape(chans, NK, seg)
-            near = (dot(near_hi, near_one) + dot(near_lo, near_one)).reshape(chans, NK, seg)
+            near = dot(near_gain, near_two).reshape(chans, NK, seg)
             far_re, far_im = far[:, :ND], far[:, ND:]
             near_re, near_im = near[:, :ND], near[:, ND:]
             prod_re = model_re * far_re + model_im * far_im
@@ -218,15 +229,16 @@
         return dot(cross, near_one, NT), dot(power, near_one, NT)
 
     for it in range(ITERS):
-        near_hi = near_lo = None
+        near_gain = None
         if it > 0:
             flat = gains[...].reshape(rows, owned)
             near_hi = flat.astype(BF16)
             near_lo = (flat - near_hi.astype(F32)).astype(BF16)
+            near_gain = jnp.concatenate([near_hi, near_lo], axis=1)
 
             def take_gains(i, carry):
                 s = back(i)
-                gain_copy(it - 1, s, s, s, s).wait_recv()
+                gain_copy(it - 1, s, s, s).wait_recv()
                 return carry
 
             lax.fori_loop(0, n_bl - 1, take_gains, 0)
@@ -241,7 +253,7 @@
                 def _():
                     copy3(s, s, s, s, s).wait_recv()
 
-            more = terms(it, s, near_hi, near_lo)
+            more = terms(it, s, near_gain)
             return sums[0] + more[0], sums[1] + more[1]
 
         zeros = (jnp.zeros((rows, owned), F32), jnp.zeros((chans * ND, owned), F32))
@@ -263,16 +275,14 @@
             out[...] = gain
         else:
             gains[...] = gain
-            turned = gain.reshape(rows, owned).T.astype(g_send.dtype)
-            g_send[it] = turned
+            g_all[it, b] = gain.reshape(rows, owned).T.astype(g_all.dtype)
 
             def spread(i, carry):
                 j = at(i)
-                gain_copy(it, b, j, b, j).start()
+                gain_copy(it, b, j, j).start()
                 return carry
 
             lax.fori_loop(0, n_bl - 1, spread, 0)
-            g_all[it, b] = turned
 
     for it in range(ITERS):
         for side in range(2):
@@ -283,7 +293,7 @@
         pair_copy(j, b, j, b, j).wait_send()
         copy3(j, b, j, b, j).wait_send()
         for it in range(ITERS - 1):
-            gain_copy(it, b, j, b, j).wait_send()
+            gain_copy(it, b, j, j).wait_send()
         return carry
 
     lax.fori_loop(0, n_bl - 1, drain, 0)
@@ -329,13 +339,13 @@
             pltpu.VMEM((n_bl, rows + 2 * chans, seg), BF16),
             pltpu.VMEM((n_bl, 2, seg), jnp.int32),
             pltpu.VMEM((n_bl, stations, seg), BF16),
-            pltpu.VMEM((n_bl, owned, seg), BF16),
+            pltpu.VMEM((n_bl, 2 * owned, seg), BF16),
             pltpu.VMEM((chans, NK, owned), F32),
             pltpu.VMEM((ITERS, chans, NK, owned), F32),
             pltpu.VMEM((ITERS, 2, NK, owned), F32),
-            pltpu.VMEM((ITERS - 1, owned, rows), gdt),
             pltpu.VMEM((ITERS - 1, n_bl, owned, rows), gdt),
             pltpu.VMEM((rows, stations), BF16),
+            pltpu.VMEM((stations, 1), jnp.int32),
         ]
         + [dma((n_bl,))] * 8
         + [dma((ITERS - 1, n_bl))] * 2
@@ -344,7 +354,7 @@
             collective_id=0, has_side_effects=True, vmem_limit_bytes=60 * 1024 * 1024
         ),
         name="calibrate",
-    )(tile_of, facet, kern, obs, flag, pair, solver_order.reshape(stations, 1))
+    )(tile_of, facet, kern, obs, flag, pair, solver_order.reshape(1, stations))
     return gains.reshape(chans, 2, ND, owned).transpose(0, 2, 1, 3).reshape(chans, NK, owned)
 
 

time: 96.3 us -> 95.8 us (level)
  local copies, waits for them, and re-layouts: 6.41 us -> 4.87 us
  Pallas kernels: 89.7 us -> 90.7 us
    reshape x1 -> x0, local copies, waits for them, and re-layouts: 1.52 us -> none  [body(): solver_order.reshape(stations, 1)]
    pallas_call x1, Pallas kernels: 89.7 us -> 90.7 us  [body(): pl.pallas_call(functools.partial(fused, n_bl, n_ch, tiles), out_shape=jax...]
where the time goes in v2:
time: 95.8 us; the launch traced here: 95.6 us
  Pallas kernels  90.7 us (95%)
  local copies, waits for them, and re-layouts  4.87 us (5%)
    pallas_call x1, Pallas kernels, body(): pl.pallas_call(functools.partial(fused, n_bl, n_ch, tiles), out_shape=jax...  90.7 us

profile of v2, /device:TPU:0, one launch (start us, length us, event | category | flops | bytes accessed | tf_op | source)
XLA Modules:
  0.0 95.6 jit_solution(8279781188034725643)
XLA Ops:
  0.0 1.0 %reshape.29 = bf16[16,2,8,256]{3,2,1,0:T(8,128)(2,1)S(1)} reshape(bf16[16,2,2048]{2,1,0:T(2,128)(2,1)} %param.10) | data formatting | bytes 262144 | tf_op jit(solution)/shard_map/reshape | solution.py:322
  1.0 0.7 copy.10
  1.7 1.5 %copy.15 = s32[2,8,8,256]{3,2,0,1:T(8,128)} copy(s32[2,8,8,256]{3,2,1,0:T(8,128)} %bitcast.25) | data formatting | bytes 262144 | tf_op jit(solution)/shard_map/reshape | solution.py:323
  3.2 90.7 %calibrate.1 = f32[16,16,64]{2,1,0:T(8,128)} custom-call(s32[4]{0:T(128)} %tile_of.1, bf16[4,4,256,256]{3,2,1,0:T(8,128)(2,1)} %bitcast.20, bf16[8,256,256]{2,1,0:T(8,128)(2,1)} %bitcast.21, bf16[8,32,256]{2,1,0:T(8,128)(2,1)} %bitcast.22, s32[8,16,256]{2,1,0:T(8,128)} %bitcast.24, s32[8,2,256]{2,1,0:T(2,128)} %bitcast.26, s32[1,512]{1,0:T(1,128)} %bitcast.27), custom_call_target="tpu_custom_call" | custom-call | tf_op jit(solution)/shard_map/calibrate/pallas_call | solution.py:327
  94.0 1.6 %copy.12 = f32[16,8,2,64]{3,2,1,0:T(2,128)} copy(f32[16,8,2,64]{3,1,2,0:T(8,128)} %bitcast.23) | data formatting | bytes 131072 | tf_op jit(solution)/shard_map/transpose | solution.py:358
